TPU v7x, 256 devices: a whole 4x4x8 slice. The times are simulated.
256 devices in a mesh: tgt: 8 (over y, core), src: 32 (over x, z).
Axes of the slice: x: 4, y: 4, z: 8, core: 2. Of those that a mesh axis runs over, the one named last changes fastest.
Arguments:
- queries: bfloat16 [4096, 1024], P(('tgt', 'src')), may hold values from -6 to 6
- keys: bfloat16 [8192, 1024], P('src'), may hold values from -6 to 6
- values: bfloat16 [8192, 1024], P('src'), may hold values from -6 to 6
- grad_out: bfloat16 [4096, 1024], P(('tgt', 'src')), may hold values from -6 to 6
- read_len: int32 [4096], P('tgt'), may hold values from 128 to 8192, as said below
Outputs:
- grad_queries: float32 [4096, 1024], P(('tgt', 'src'))
- grad_keys: float32 [8192, 1024], P('src', 'tgt')
- grad_values: float32 [8192, 1024], P('src', 'tgt')
Inputs may be any that keep to these rules, and one draw needn't show every extreme that they name: `read_len`: multiples of 128, never falling along the target tokens; the first token reads 128 frames and the last reads all 8192.
All inputs are finite; a program needn't handle non-finite values.
Results may differ from a plain program's by a relative error of at most 0.008.
Values may be sent and summed in bfloat16 or wider, within the bound.
A program may use at most 64 MiB of HBM per device.

v0:
```python
import jax
import jax.numpy as jnp
from jax import lax
from jax.experimental import pallas as pl
from jax.experimental.pallas import tpu as pltpu
from jax.sharding import PartitionSpec as P

MESH = pl.DeviceIdType.MESH
NX, NZ = 4, 8
COLS = 128
MASK_BLOCK = 128
F32, BF16 = jnp.float32, jnp.bfloat16
HIDDEN = -1e30
SCALE = 0.125

REL = [0]
for _d in range(1, NZ // 2 + 1):
    REL += [_d] if 2 * _d == NZ else [_d, NZ - _d]
POS = {d: p for p, d in enumerate(REL)}


def kernel(
    NT, q_hbm, k_hbm, v_hbm, g_hbm, len_hbm, dq_out, dk_out, dv_out,
    len_ref, QI, GI, QGI, QG, KV, L, lrow, M, K2, V2, KT, W, G, MR, SM, SR, CF, RT, PS, GS, Q2, G2, DQT, DQS, DQR, DK, DV, DKVS, DKVR,
    lsem, as_, ar, bs, br, cs, cr, ds_, dr, es, er, fs, fr, gs, gr,
):
    t = lax.axis_index("tgt")
    s = lax.axis_index("src")
    x = s // NZ
    z = s % NZ
    R, F = q_hbm.shape[0], k_hbm.shape[0]
    TOK = NT * R
    CH = 2 * TOK
    NC = NZ // 2

    def tpeer(d):
        return (lax.rem(t + d, NT), s)

    def zpeer(d):
        return (t, x * NZ + lax.rem(z + NZ + d, NZ))

    def diagonal(i, d):
        return (lax.rem(t + i, NT), x * NZ + lax.rem(z + NZ + d, NZ))

    def xpeer(d):
        return (t, lax.rem(x + d, NX) * NZ + z)

    def cols(i):
        return pl.ds(pl.multiple_of(i * COLS, COLS), COLS)

    def remote(src, dst, ssem, rsem, dev):
        return pltpu.make_async_remote_copy(
            src_ref=src, dst_ref=dst, send_sem=ssem, recv_sem=rsem, device_id=dev, device_id_type=MESH
        )

    local = [
        pltpu.make_async_copy(q_hbm, QI, lsem.at[0]),
        pltpu.make_async_copy(g_hbm, GI, lsem.at[1]),
        pltpu.make_async_copy(k_hbm.at[:, cols(t)], KV.at[0, 0], lsem.at[2]),
        pltpu.make_async_copy(v_hbm.at[:, cols(t)], KV.at[0, 1], lsem.at[3]),
        pltpu.make_async_copy(len_hbm, len_ref, lsem.at[4]),
    ]
    for copy in local:
        copy.start()
    barrier = pltpu.get_barrier_semaphore()
    peers = [tpeer(d) for d in range(1, NT)] + [diagonal(i, d) for i in range(1, NT) for d in (1, -1, 2, -2)]
    peers += [zpeer(d) for d in range(1, NZ)] + [xpeer(d) for d in range(1, NX)]
    for dev in peers:
        pl.semaphore_signal(barrier, inc=1, device_id=dev, device_id_type=MESH)
    pl.semaphore_wait(barrier, len(peers))

    for copy in local:
        copy.wait()
    row = len_ref[pl.ds(x, 1), :].astype(F32)
    lrow[...] = jnp.broadcast_to(row, lrow.shape)
    L[pl.ds(t, 1)] = jnp.broadcast_to(row[None], (1,) + lrow.shape)
    sent = []
    for i in range(NT):
        QGI[i, 0] = QI[:, i * COLS : (i + 1) * COLS]
        QGI[i, 1] = GI[:, i * COLS : (i + 1) * COLS]
    def straight(slot, d):
        for i in range(NT):
            remote(QGI.at[lax.rem(t + i, NT)], QG.at[slot, :, t], bs.at[0, slot], br.at[0, slot], diagonal(i, d)).start()

    def share(d):
        for part in range(2):
            sent.append(remote(KV.at[0, part], KV.at[NX - d, part], cs.at[part, d], cr.at[part, NX - d], xpeer(d)))

    straight(2, 1)
    straight(1, -1)
    share(1)
    share(NX - 1)
    for d in range(1, NT):
        sent.append(remote(lrow, L.at[t], as_.at[1, d], ar.at[1, d], tpeer(d)))
    for d in range(1, NT):
        sent.append(remote(QGI.at[lax.rem(t + d, NT)], QG.at[0, :, t], as_.at[0, d], ar.at[0, d], tpeer(d)))
    for copy in sent:
        copy.start()
    straight(4, 2)
    straight(3, -2)
    share(NX // 2)
    for copy in sent[-2:]:
        copy.start()
    for part in range(2):
        QG[0, part, pl.ds(t, 1)] = QGI[pl.ds(t, 1), part]

    onward = [
        remote(QG.at[4], QG.at[6], bs.at[0, 6], br.at[0, 6], zpeer(1)),
        remote(QG.at[3], QG.at[5], bs.at[0, 5], br.at[0, 5], zpeer(-1)),
        remote(QG.at[4, 1], QG.at[7, 1], bs.at[1, 7], br.at[1, 7], zpeer(2)),
        remote(QG.at[3, 0], QG.at[7, 0], bs.at[0, 7], br.at[0, 7], zpeer(-2)),
    ]

    def arrived(slot):
        remote(QG.at[0], QG.at[slot], bs.at[0, 3], br.at[0, slot], zpeer(1)).wait_recv()

    lane2 = lax.broadcasted_iota(jnp.int32, (1, COLS), 1)
    head = [(lane2 < COLS // 2).astype(F32), (lane2 >= COLS // 2).astype(F32)]
    rows2 = lax.broadcasted_iota(jnp.int32, (F, COLS), 0)
    lanes2 = lax.broadcasted_iota(jnp.int32, (F, COLS), 1)
    per = F // MASK_BLOCK

    def build(r):
        kb = KV[r, 0].astype(F32)
        vb = KV[r, 1].astype(F32)
        hot = (lanes2 == rows2 // MASK_BLOCK + per * r).astype(F32).astype(BF16)
        for h in range(2):
            kh = kb * (head[h] * SCALE)
            K2[r, h * F : (h + 1) * F, 0:COLS] = kh.astype(BF16)
            K2[r, h * F : (h + 1) * F, COLS : 2 * COLS] = hot
            V2[r, h * F : (h + 1) * F, :] = (vb * head[h]).astype(BF16)
            KT[r, :, h * F : (h + 1) * F] = kh.T.astype(BF16)

    build(0)
    for d in range(1, NT):
        source = lax.rem(t + NT - d, NT)
        remote(lrow, L.at[source], as_.at[1, d], ar.at[1, d], tpeer(d)).wait_recv()
    lane3 = lax.broadcasted_iota(jnp.int32, (NT, R, COLS), 2)
    row3 = lax.broadcasted_iota(jnp.int32, (NT, R, COLS), 1)
    lens = jnp.broadcast_to(L[:, 0:1, :], (NT, R, COLS))
    lanes = lax.broadcasted_iota(jnp.int32, (1, 1, COLS), 2)
    first = ((lax.rem(x + lanes // per, NX) * NZ + z) * per + lax.rem(lanes, per)) * MASK_BLOCK
    first = jnp.where(lanes < per * NX, first, -1).astype(F32)

    def mask_slot(p, rel):
        pick = lax.rem(z + rel, NZ) * R + row3
        column = jnp.sum(jnp.where(lane3 == pick, lens, 0.0), axis=2, keepdims=True)
        M[p] = jnp.where(first >= column, HIDDEN, 0.0).reshape(TOK, COLS).T.astype(BF16)

    for p in range(NZ):
        mask_slot(p, REL[p])

    for d in range(1, NT):
        source = lax.rem(t + NT - d, NT)
        remote(QGI.at[0], QG.at[0, :, source], as_.at[0, d], ar.at[0, d], tpeer(d)).wait_recv()

    arrived(1)

    masks = [m.astype(BF16) for m in head]

    def block(ref, c, which):
        return ref[pl.ds(2 * c, 2), which].reshape(CH, COLS)

    def pass_on():
        for slot in (2, 3, 4):
            arrived(slot)
        for copy in onward:
            copy.start()

    def pass1(c, fresh):
        qt = jnp.concatenate([block(QG, c, 0).T, jnp.concatenate([M[2 * c], M[2 * c + 1]], axis=1)], axis=0)
        gt = block(QG, c, 1).T
        for h in range(2):
            rows = slice(h * CH, (h + 1) * CH)
            Q2[c, rows] = block(QG, c, 0) * masks[h]
            G2[c, rows] = block(QG, c, 1) * masks[h]
        found = [[] for _ in range(4)]

        def products(r, h):
            rows = slice(h * F, (h + 1) * F)
            W[c, r, h] = jnp.dot(K2[r, rows], qt, preferred_element_type=F32)
            G[c, r, h] = jnp.dot(V2[r, rows], gt, preferred_element_type=F32)

        def reduce(r, h):
            for half in range(2):
                piece = slice(half * TOK, (half + 1) * TOK)
                sc = W[c, r, h, :, piece]
                m = jnp.max(sc, axis=0, keepdims=True)
                w = jnp.exp(sc - m)
                W[c, r, h, :, piece] = w
                MR[c, 2 * r + h : 2 * r + h + 1, piece] = m
                l = jnp.sum(w, axis=0, keepdims=True)
                found[2 * h + half].append((m, l, jnp.sum(w * G[c, r, h, :, piece], axis=0, keepdims=True)))

        order = [(r, h) for r in (0, 1, NX - 1, NX // 2) for h in range(2)]
        products(*order[0])
        for now, later in zip(order, order[1:] + [None]):
            wait = fresh and later is not None and later[1] == 0
            if wait:
                reduce(*now)
                r = later[0]
                if r == NX // 2:
                    pass_on()
                for part in range(2):
                    remote(KV.at[0, part], KV.at[r, part], cs.at[part, r], cr.at[part, r], xpeer(r)).wait_recv()
                build(r)
            if later is not None:
                products(*later)
            if not wait:
                reduce(*now)
        for h in range(2):
            for half in range(2):
                top = found[2 * h + half][0][0]
                for m, _, _ in found[2 * h + half][1:]:
                    top = jnp.maximum(top, m)
                total = jnp.zeros_like(top)
                term = jnp.zeros_like(top)
                for m, l, tt in found[2 * h + half]:
                    a = jnp.exp(m - top)
                    total += a * l
                    term += a * tt
                row = 2 * half + h
                SM[c, row : row + 1, :] = top + jnp.log(total)
                SM[c, 4 + row : 5 + row, :] = term / total
        for d in REL[1:]:
            remote(SM.at[c], SR.at[NZ - d, c], ds_.at[d], dr.at[NZ - d], zpeer(d)).start()

        @pl.when(c == 1)
        def _():
            arrived(5)

        @pl.when(c == 2)
        def _():
            arrived(6)
            for part in range(2):
                onward[3 - part].wait_recv()

        return 0

    pass1(0, True)
    lax.fori_loop(1, NC, lambda c, _: pass1(c, False), 0)

    for d in range(1, NZ):
        remote(SM, SR.at[d], ds_.at[d], dr.at[d], zpeer(d)).wait_recv()

    def combine(p):
        parts, terms = [], []
        for d in range(NZ):
            theirs = POS[(REL[p] - d) % NZ]
            ref = SM if d == 0 else SR.at[d]
            row = 2 * (theirs % 2)
            parts.append(ref[theirs // 2, row : row + 2, :])
            terms.append(ref[theirs // 2, 4 + row : 6 + row, :])
        top = parts[0]
        for part in parts[1:]:
            top = jnp.maximum(top, part)
        total = jnp.zeros_like(top)
        term = jnp.zeros_like(top)
        for part, other in zip(parts, terms):
            weight = jnp.exp(part - top)
            total += weight
            term += weight * other
        CF[:, p * TOK : (p + 1) * TOK] = top + jnp.log(total)
        RT[:, p * TOK : (p + 1) * TOK] = term / total

    for p in range(NZ):
        combine(p)

    def make(c, r):
        piece = slice(c * CH, (c + 1) * CH)
        for h in range(2):
            cf = jnp.exp(MR[c, 2 * r + h : 2 * r + h + 1, :] - CF[h : h + 1, piece])
            term = RT[h : h + 1, piece]
            for lo in range(0, F, 64):
                rows = slice(lo, lo + 64)
                p = W[c, r, h, rows, :] * cf
                PS[c, r, rows, h * CH : (h + 1) * CH] = p.astype(BF16)
                GS[c, r, rows, h * CH : (h + 1) * CH] = (p * (G[c, r, h, rows, :] - term)).astype(BF16)

    def use(c, r):
        first = c == NC - 1
        dv = jnp.dot(PS[c, r], G2[c], preferred_element_type=F32)
        dk = jnp.dot(GS[c, r], Q2[c], preferred_element_type=F32)
        DV[r] = dv if first else DV[r] + dv
        DK[r] = dk if first else DK[r] + dk
        dq = jnp.dot(KT[r, :, 0:F], GS[c, r, :, 0:CH], preferred_element_type=F32)
        dq += jnp.dot(KT[r, :, F : 2 * F], GS[c, r, :, CH : 2 * CH], preferred_element_type=F32)
        DQT[c] = dq if r == ORDER[0] else DQT[c] + dq

    def send_dq(p):
        d = REL[p]
        for i in range(NT):
            if p > 0 or i > 0:
                there = lax.rem(t + i, NT)
                remote(
                    DQS.at[p, there], DQR.at[(NZ - d) % NZ, t],
                    es.at[d] if d else gs.at[i], er.at[(NZ - d) % NZ] if d else gr.at[i],
                    (there, x * NZ + lax.rem(z + d, NZ)),
                ).start()

    def done_dq(c):
        DQS[2 * c : 2 * c + 2] = DQT[c].T.astype(BF16).reshape(2, NT, R, COLS)
        send_dq(2 * c + 1)
        send_dq(2 * c)

    def done_kv(r):
        DKVS[r, 0] = DK[r].astype(BF16)
        DKVS[r, 1] = DV[r].astype(BF16)
        sent.append(remote(DKVS.at[r], DKVR.at[NX - r], fs.at[r], fr.at[NX - r], xpeer(r)))
        sent[-1].start()

    ORDER = [NX // 2] + [i for i in range(1, NX) if i != NX // 2] + [0]
    steps = [(c, r) for c in range(NC - 1, 1, -1) for r in ORDER] + [(c, r) for r in ORDER for c in (1, 0)]
    make(*steps[0])
    for (c, r), later in zip(steps, steps[1:] + [None]):
        if later is not None:
            make(*later)
        use(c, r)
        if r == ORDER[-1]:
            done_dq(c)
        if c == 0 and r > 0:
            done_kv(r)
    DQR[0, pl.ds(t, 1)] = DQS[0, pl.ds(t, 1)]

    for d in range(1, NX):
        remote(DKVS.at[d], DKVR.at[d], fs.at[d], fr.at[d], xpeer(d)).wait_recv()
    dk, dv = DK[0], DV[0]
    for d in range(1, NX):
        dk += DKVR[d, 0].astype(F32)
        dv += DKVR[d, 1].astype(F32)
    dk_out[...] = dk * SCALE
    dv_out[...] = dv

    for d in range(1, NT):
        source = lax.rem(t + NT - d, NT)
        remote(DQS.at[0, 0], DQR.at[0, source], gs.at[d], gr.at[d], tpeer(d)).wait_recv()
    for d in range(1, NZ):
        remote(DQS.at[POS[d]], DQR.at[d], es.at[d], er.at[d], zpeer(d)).wait_recv()
    for i in range(NT):
        dq = DQR[0, i].astype(F32)
        for d in range(1, NZ):
            dq += DQR[d, i].astype(F32)
        dq_out[:, i * COLS : (i + 1) * COLS] = dq
    for copy in sent:
        copy.wait_send()
    for slot in range(1, 5):
        remote(QGI, QG.at[slot], bs.at[0, slot], br.at[0, slot], zpeer(1)).wait_send()
    for copy in onward:
        copy.wait_send()
    for d in range(1, NT):
        remote(DQS.at[0, 0], DQR.at[0, 0], gs.at[d], gr.at[d], tpeer(d)).wait_send()
    for d in range(1, NZ):
        remote(DQS.at[POS[d]], DQR.at[d], es.at[d], er.at[d], zpeer(d)).wait_send()
    for d in range(1, NZ):
        remote(SM, SR.at[NZ - d], ds_.at[d], dr.at[NZ - d], zpeer(d)).wait_send()


def body(queries, keys, values, grad_out, read_len, *, NT):
    R, D = queries.shape
    F = keys.shape[0]
    TOK, CH, NC = NT * R, 2 * NT * R, NZ // 2
    lens = read_len.reshape(NX, NZ * R)
    hbm = pl.BlockSpec(memory_space=pltpu.HBM)
    vmem = pl.BlockSpec(memory_space=pltpu.VMEM)
    dma = pltpu.SemaphoreType.DMA
    V = pltpu.VMEM
    return pl.pallas_call(
        lambda *refs: kernel(NT, *refs),
        out_shape=(V((R, D), F32), V((F, COLS), F32), V((F, COLS), F32)),
        in_specs=[hbm] * 5,
        out_specs=(vmem, vmem, vmem),
        scratch_shapes=[
            V((NX, NZ * R), jnp.int32),
            V((R, D), BF16),
            V((R, D), BF16),
            V((NT, 2, R, COLS), BF16),
            V((NZ, 2, NT, R, COLS), BF16),
            V((NX, 2, F, COLS), BF16),
            V((NT, 8, COLS), F32),
            V((8, COLS), F32),
            V((NZ, COLS, TOK), BF16),
            V((NX, 2 * F, 2 * COLS), BF16),
            V((NX, 2 * F, COLS), BF16),
            V((NX, COLS, 2 * F), BF16),
            V((NC, NX, 2, F, CH), F32),
            V((NC, NX, 2, F, CH), F32),
            V((NC, 2 * NX, CH), F32),
            V((NC, 8, TOK), F32),
            V((NZ, NC, 8, TOK), F32),
            V((2, NZ * TOK), F32),
            V((2, NZ * TOK), F32),
            V((NC, NX, F, 2 * CH), BF16),
            V((NC, NX, F, 2 * CH), BF16),
            V((NC, 2 * CH, COLS), BF16),
            V((NC, 2 * CH, COLS), BF16),
            V((NC, COLS, CH), F32),
            V((NZ, NT, R, COLS), BF16),
            V((NZ, NT, R, COLS), BF16),
            V((NX, F, COLS), F32),
            V((NX, F, COLS), F32),
            V((NX, 2, F, COLS), BF16),
            V((NX, 2, F, COLS), BF16),
            dma((5,)),
            dma((2, NT)), dma((2, NT)),
            dma((2, NZ)), dma((2, NZ)),
            dma((2, NX)), dma((2, NX)),
            dma((NZ,)), dma((NZ,)),
            dma((NZ,)), dma((NZ,)),
            dma((NX,)), dma((NX,)),
            dma((NT,)), dma((NT,)),
        ],
        compiler_params=pltpu.CompilerParams(
            collective_id=0, has_side_effects=True, vmem_limit_bytes=62 * 1024 * 1024
        ),
    )(queries, keys, values, grad_out, lens)


def solution(mesh):
    NT = mesh.shape["tgt"]
    return jax.shard_map(
        lambda *args: body(*args, NT=NT),
        mesh=mesh,
        in_specs=(
            P(("tgt", "src"), None),
            P("src", None),
            P("src", None),
            P(("tgt", "src"), None),
            P("tgt"),
        ),
        out_specs=(P(("tgt", "src"), None), P("src", "tgt"), P("src", "tgt")),
        check_vma=False,
    )
```

profile of v0, /device:TPU:1, one launch (start us, length us, event | category | flops | bytes accessed | tf_op | source)
XLA Modules:
  0.0 44.0 jit_solution(13633703200925701455)
XLA Ops:
  0.6 41.4 %shard_map.76 = (f32[16,1024]{1,0:T(8,128)S(1)}, f32[256,128]{1,0:T(8,128)S(1)}, f32[256,128]{1,0:T(8,128)S(1)}) custom-call(bf16[16,1024]{1,0:T(8,128)(2,1)} %refs_0_.1, bf16[256,1024]{1,0:T(8,128)(2,1)} %refs_1_.1, bf16[256,1024]{1,0:T(8,128)(2,1)} %refs_2_.1, bf16[16,1024]{1,0:T(8,128)(2,1)} %refs_3_.1, s32[4,128]{1,0:T(4,128)} %bitcast.1), custom_call_target="tpu_custom_call" | custom-call | tf_op jit(solution)/shard_map/pallas_call | solution.py:367
  42.1 0.6 %copy.11 = f32[16,1024]{1,0:T(8,128)} copy(f32[16,1024]{1,0:T(8,128)S(1)} %get-tuple-element.3) | data formatting | bytes 131072
  42.7 0.7 %copy.12 = f32[256,128]{1,0:T(8,128)} copy(f32[256,128]{1,0:T(8,128)S(1)} %get-tuple-element.4) | data formatting | bytes 262144
  43.3 0.7 %copy.13 = f32[256,128]{1,0:T(8,128)} copy(f32[256,128]{1,0:T(8,128)S(1)} %get-tuple-element.5) | data formatting | bytes 262144
where the time goes:
time: 44.1 us; the launch traced here: 44 us
  Pallas kernels  41.4 us (94%)
  local copies, waits for them, and re-layouts  1.94 us (4%)
  between operations  0.64 us (1%)
    pallas_call x1, Pallas kernels, body(): pl.pallas_call(lambda *refs: kernel(NT, *refs), out_shape=(V((R, D), F32)...  41.4 us
    unnamed x3, local copies, waits for them, and re-layouts  1.94 us

commit v1 on v0

--- a/solution.py
+++ b/solution.py
@@ -263,8 +263,6 @@
         CF[:, p * TOK : (p + 1) * TOK] = top + jnp.log(total)
         RT[:, p * TOK : (p + 1) * TOK] = term / total
 
-    for p in range(NZ):
-        combine(p)
 
     def make(c, r):
         piece = slice(c * CH, (c + 1) * CH)
@@ -311,7 +309,13 @@
 
     ORDER = [NX // 2] + [i for i in range(1, NX) if i != NX // 2] + [0]
     steps = [(c, r) for c in range(NC - 1, 1, -1) for r in ORDER] + [(c, r) for r in ORDER for c in (1, 0)]
+    early = list(sent)
+    sent.clear()
+    combine(NZ - 2)
+    combine(NZ - 1)
     make(*steps[0])
+    for p in range(NZ - 2):
+        combine(p)
     for (c, r), later in zip(steps, steps[1:] + [None]):
         if later is not None:
             make(*later)
@@ -322,6 +326,14 @@
             done_kv(r)
     DQR[0, pl.ds(t, 1)] = DQS[0, pl.ds(t, 1)]
 
+    for copy in early:
+        copy.wait_send()
+    for slot in range(1, 5):
+        remote(QGI, QG.at[slot], bs.at[0, slot], br.at[0, slot], zpeer(1)).wait_send()
+    for copy in onward:
+        copy.wait_send()
+    for d in range(1, NZ):
+        remote(SM, SR.at[NZ - d], ds_.at[d], dr.at[NZ - d], zpeer(d)).wait_send()
     for d in range(1, NX):
         remote(DKVS.at[d], DKVR.at[d], fs.at[d], fr.at[d], xpeer(d)).wait_recv()
     dk, dv = DK[0], DV[0]
@@ -343,16 +355,10 @@
         dq_out[:, i * COLS : (i + 1) * COLS] = dq
     for copy in sent:
         copy.wait_send()
-    for slot in range(1, 5):
-        remote(QGI, QG.at[slot], bs.at[0, slot], br.at[0, slot], zpeer(1)).wait_send()
-    for copy in onward:
-        copy.wait_send()
     for d in range(1, NT):
         remote(DQS.at[0, 0], DQR.at[0, 0], gs.at[d], gr.at[d], tpeer(d)).wait_send()
     for d in range(1, NZ):
         remote(DQS.at[POS[d]], DQR.at[d], es.at[d], er.at[d], zpeer(d)).wait_send()
-    for d in range(1, NZ):
-        remote(SM, SR.at[NZ - d], ds_.at[d], dr.at[NZ - d], zpeer(d)).wait_send()
 
 
 def body(queries, keys, values, grad_out, read_len, *, NT):

time: 44.1 us -> 44 us (level)
  no operation moved by 1% of the time
where the time goes in v1:
time: 44 us; the launch traced here: 43.9 us
  Pallas kernels  41.4 us (94%)
  local copies, waits for them, and re-layouts  1.94 us (4%)
  between operations  0.64 us (1%)
    pallas_call x1, Pallas kernels, body(): pl.pallas_call(lambda *refs: kernel(NT, *refs), out_shape=(V((R, D), F32)...  41.4 us
    unnamed x3, local copies, waits for them, and re-layouts  1.94 us

profile of v1, /device:TPU:1, one launch (start us, length us, event | category | flops | bytes accessed | tf_op | source)
XLA Modules:
  0.0 43.9 jit_solution(10790869199370132352)
XLA Ops:
  0.6 41.4 %shard_map.76 = (f32[16,1024]{1,0:T(8,128)S(1)}, f32[256,128]{1,0:T(8,128)S(1)}, f32[256,128]{1,0:T(8,128)S(1)}) custom-call(bf16[16,1024]{1,0:T(8,128)(2,1)} %refs_0_.1, bf16[256,1024]{1,0:T(8,128)(2,1)} %refs_1_.1, bf16[256,1024]{1,0:T(8,128)(2,1)} %refs_2_.1, bf16[16,1024]{1,0:T(8,128)(2,1)} %refs_3_.1, s32[4,128]{1,0:T(4,128)} %bitcast.1), custom_call_target="tpu_custom_call" | custom-call | tf_op jit(solution)/shard_map/pallas_call | solution.py:373
  42.0 0.6 %copy.11 = f32[16,1024]{1,0:T(8,128)} copy(f32[16,1024]{1,0:T(8,128)S(1)} %get-tuple-element.3) | data formatting | bytes 131072
  42.6 0.7 %copy.12 = f32[256,128]{1,0:T(8,128)} copy(f32[256,128]{1,0:T(8,128)S(1)} %get-tuple-element.4) | data formatting | bytes 262144
  43.3 0.7 %copy.13 = f32[256,128]{1,0:T(8,128)} copy(f32[256,128]{1,0:T(8,128)S(1)} %get-tuple-element.5) | data formatting | bytes 262144

commit v2 on v1

--- a/solution.py
+++ b/solution.py
@@ -8,6 +8,7 @@
 MESH = pl.DeviceIdType.MESH
 NX, NZ = 4, 8
 COLS = 128
+HALF = COLS // 2
 MASK_BLOCK = 128
 F32, BF16 = jnp.float32, jnp.bfloat16
 HIDDEN = -1e30
@@ -21,7 +22,7 @@
 
 def kernel(
     NT, q_hbm, k_hbm, v_hbm, g_hbm, len_hbm, dq_out, dk_out, dv_out,
-    len_ref, QI, GI, QGI, QG, KV, L, lrow, M, K2, V2, KT, W, G, MR, SM, SR, CF, RT, PS, GS, Q2, G2, DQT, DQS, DQR, DK, DV, DKVS, DKVR,
+    len_ref, QI, GI, QGI, QG, KV, L, lrow, M, K2, KT, W, G, MR, SM, SR, CF, RT, PS, GS, Q2, G2, DQT, DQS, DQR, DK, DV, DKVS, DKVR,
     lsem, as_, ar, bs, br, cs, cr, ds_, dr, es, er, fs, fr, gs, gr,
 ):
     t = lax.axis_index("tgt")
@@ -121,15 +122,13 @@
     per = F // MASK_BLOCK
 
     def build(r):
-        kb = KV[r, 0].astype(F32)
-        vb = KV[r, 1].astype(F32)
-        hot = (lanes2 == rows2 // MASK_BLOCK + per * r).astype(F32).astype(BF16)
+        kb = KV[r, 0].astype(F32) * SCALE
+        block_of = rows2 // MASK_BLOCK + per * r
         for h in range(2):
-            kh = kb * (head[h] * SCALE)
-            K2[r, h * F : (h + 1) * F, 0:COLS] = kh.astype(BF16)
-            K2[r, h * F : (h + 1) * F, COLS : 2 * COLS] = hot
-            V2[r, h * F : (h + 1) * F, :] = (vb * head[h]).astype(BF16)
-            KT[r, :, h * F : (h + 1) * F] = kh.T.astype(BF16)
+            mine = (lanes2 < HALF) if h == 0 else (lanes2 >= HALF)
+            hot = (lanes2 == block_of + HALF * (1 - h)).astype(F32)
+            K2[r, h * F : (h + 1) * F] = jnp.where(mine, kb, hot).astype(BF16)
+        KT[r] = kb.T.astype(BF16)
 
     build(0)
     for d in range(1, NT):
@@ -145,7 +144,7 @@
     def mask_slot(p, rel):
         pick = lax.rem(z + rel, NZ) * R + row3
         column = jnp.sum(jnp.where(lane3 == pick, lens, 0.0), axis=2, keepdims=True)
-        M[p] = jnp.where(first >= column, HIDDEN, 0.0).reshape(TOK, COLS).T.astype(BF16)
+        M[p] = jnp.where(first >= column, HIDDEN, 0.0).reshape(TOK, COLS).T[0:HALF].astype(BF16)
 
     for p in range(NZ):
         mask_slot(p, REL[p])
@@ -168,8 +167,11 @@
             copy.start()
 
     def pass1(c, fresh):
-        qt = jnp.concatenate([block(QG, c, 0).T, jnp.concatenate([M[2 * c], M[2 * c + 1]], axis=1)], axis=0)
-        gt = block(QG, c, 1).T
+        qt, gt = block(QG, c, 0).T, block(QG, c, 1).T
+        mt = jnp.concatenate([M[2 * c], M[2 * c + 1]], axis=1)
+        none = jnp.zeros((HALF, CH), BF16)
+        qts = [jnp.concatenate([qt[0:HALF], mt], axis=0), jnp.concatenate([mt, qt[HALF:COLS]], axis=0)]
+        gts = [jnp.concatenate([gt[0:HALF], none], axis=0), jnp.concatenate([none, gt[HALF:COLS]], axis=0)]
         for h in range(2):
             rows = slice(h * CH, (h + 1) * CH)
             Q2[c, rows] = block(QG, c, 0) * masks[h]
@@ -178,8 +180,8 @@
 
         def products(r, h):
             rows = slice(h * F, (h + 1) * F)
-            W[c, r, h] = jnp.dot(K2[r, rows], qt, preferred_element_type=F32)
-            G[c, r, h] = jnp.dot(V2[r, rows], gt, preferred_element_type=F32)
+            W[c, r, h] = jnp.dot(K2[r, rows], qts[h], preferred_element_type=F32)
+            G[c, r, h] = jnp.dot(KV[r, 1], gts[h], preferred_element_type=F32)
 
         def reduce(r, h):
             for half in range(2):
@@ -281,9 +283,10 @@
         dk = jnp.dot(GS[c, r], Q2[c], preferred_element_type=F32)
         DV[r] = dv if first else DV[r] + dv
         DK[r] = dk if first else DK[r] + dk
-        dq = jnp.dot(KT[r, :, 0:F], GS[c, r, :, 0:CH], preferred_element_type=F32)
-        dq += jnp.dot(KT[r, :, F : 2 * F], GS[c, r, :, CH : 2 * CH], preferred_element_type=F32)
-        DQT[c] = dq if r == ORDER[0] else DQT[c] + dq
+        for h in range(2):
+            out = slice(h * HALF, (h + 1) * HALF)
+            dq = jnp.dot(KT[r, out], GS[c, r, :, h * CH : (h + 1) * CH], preferred_element_type=F32)
+            DQT[c, out] = dq if r == ORDER[0] else DQT[c, out] + dq
 
     def send_dq(p):
         d = REL[p]
@@ -384,10 +387,9 @@
             V((NX, 2, F, COLS), BF16),
             V((NT, 8, COLS), F32),
             V((8, COLS), F32),
-            V((NZ, COLS, TOK), BF16),
-            V((NX, 2 * F, 2 * COLS), BF16),
+            V((NZ, HALF, TOK), BF16),
             V((NX, 2 * F, COLS), BF16),
-            V((NX, COLS, 2 * F), BF16),
+            V((NX, COLS, F), BF16),
             V((NC, NX, 2, F, CH), F32),
             V((NC, NX, 2, F, CH), F32),
             V((NC, 2 * NX, CH), F32),

time: 44 us -> 43.7 us (level)
  no operation moved by 1% of the time
where the time goes in v2:
time: 43.7 us; the launch traced here: 43.6 us
  Pallas kernels  41 us (94%)
  local copies, waits for them, and re-layouts  1.94 us (4%)
  between operations  0.64 us (1%)
    pallas_call x1, Pallas kernels, body(): pl.pallas_call(lambda *refs: kernel(NT, *refs), out_shape=(V((R, D), F32)...  41 us
    unnamed x3, local copies, waits for them, and re-layouts  1.94 us

profile of v2, /device:TPU:1, one launch (start us, length us, event | category | flops | bytes accessed | tf_op | source)
XLA Modules:
  0.0 43.6 jit_solution(6016536803290501335)
XLA Ops:
  0.6 41.0 %shard_map.76 = (f32[16,1024]{1,0:T(8,128)S(1)}, f32[256,128]{1,0:T(8,128)S(1)}, f32[256,128]{1,0:T(8,128)S(1)}) custom-call(bf16[16,1024]{1,0:T(8,128)(2,1)} %refs_0_.1, bf16[256,1024]{1,0:T(8,128)(2,1)} %refs_1_.1, bf16[256,1024]{1,0:T(8,128)(2,1)} %refs_2_.1, bf16[16,1024]{1,0:T(8,128)(2,1)} %refs_3_.1, s32[4,128]{1,0:T(4,128)} %bitcast.1), custom_call_target="tpu_custom_call" | custom-call | tf_op jit(solution)/shard_map/pallas_call | solution.py:376
  41.7 0.6 %copy.11 = f32[16,1024]{1,0:T(8,128)} copy(f32[16,1024]{1,0:T(8,128)S(1)} %get-tuple-element.3) | data formatting | bytes 131072
  42.3 0.7 %copy.12 = f32[256,128]{1,0:T(8,128)} copy(f32[256,128]{1,0:T(8,128)S(1)} %get-tuple-element.4) | data formatting | bytes 262144
  43.0 0.7 %copy.13 = f32[256,128]{1,0:T(8,128)} copy(f32[256,128]{1,0:T(8,128)S(1)} %get-tuple-element.5) | data formatting | bytes 262144

commit v3 on v2

--- a/solution.py
+++ b/solution.py
@@ -146,7 +146,7 @@
         column = jnp.sum(jnp.where(lane3 == pick, lens, 0.0), axis=2, keepdims=True)
         M[p] = jnp.where(first >= column, HIDDEN, 0.0).reshape(TOK, COLS).T[0:HALF].astype(BF16)
 
-    for p in range(NZ):
+    for p in range(2):
         mask_slot(p, REL[p])
 
     for d in range(1, NT):
@@ -161,10 +161,12 @@
         return ref[pl.ds(2 * c, 2), which].reshape(CH, COLS)
 
     def pass_on():
-        for slot in (2, 3, 4):
-            arrived(slot)
-        for copy in onward:
-            copy.start()
+        arrived(4)
+        onward[0].start()
+        onward[2].start()
+        arrived(3)
+        onward[1].start()
+        onward[3].start()
 
     def pass1(c, fresh):
         qt, gt = block(QG, c, 0).T, block(QG, c, 1).T
@@ -203,6 +205,9 @@
                 r = later[0]
                 if r == NX // 2:
                     pass_on()
+                    for p in range(2, NZ):
+                        mask_slot(p, REL[p])
+                    arrived(2)
                 for part in range(2):
                     remote(KV.at[0, part], KV.at[r, part], cs.at[part, r], cr.at[part, r], xpeer(r)).wait_recv()
                 build(r)

time: 43.7 us -> 43.7 us (level)
  no operation moved by 1% of the time
where the time goes in v3:
time: 43.7 us; the launch traced here: 43.6 us
  Pallas kernels  41 us (94%)
  local copies, waits for them, and re-layouts  1.94 us (4%)
  between operations  0.64 us (1%)
    pallas_call x1, Pallas kernels, body(): pl.pallas_call(lambda *refs: kernel(NT, *refs), out_shape=(V((R, D), F32)...  41 us
    unnamed x3, local copies, waits for them, and re-layouts  1.94 us

profile of v3, /device:TPU:1, one launch (start us, length us, event | category | flops | bytes accessed | tf_op | source)
XLA Modules:
  0.0 43.6 jit_solution(7061817028846871219)
XLA Ops:
  0.6 41.0 %shard_map.76 = (f32[16,1024]{1,0:T(8,128)S(1)}, f32[256,128]{1,0:T(8,128)S(1)}, f32[256,128]{1,0:T(8,128)S(1)}) custom-call(bf16[16,1024]{1,0:T(8,128)(2,1)} %refs_0_.1, bf16[256,1024]{1,0:T(8,128)(2,1)} %refs_1_.1, bf16[256,1024]{1,0:T(8,128)(2,1)} %refs_2_.1, bf16[16,1024]{1,0:T(8,128)(2,1)} %refs_3_.1, s32[4,128]{1,0:T(4,128)} %bitcast.1), custom_call_target="tpu_custom_call" | custom-call | tf_op jit(solution)/shard_map/pallas_call | solution.py:381
  41.7 0.6 %copy.11 = f32[16,1024]{1,0:T(8,128)} copy(f32[16,1024]{1,0:T(8,128)S(1)} %get-tuple-element.3) | data formatting | bytes 131072
  42.3 0.7 %copy.12 = f32[256,128]{1,0:T(8,128)} copy(f32[256,128]{1,0:T(8,128)S(1)} %get-tuple-element.4) | data formatting | bytes 262144
  43.0 0.7 %copy.13 = f32[256,128]{1,0:T(8,128)} copy(f32[256,128]{1,0:T(8,128)S(1)} %get-tuple-element.5) | data formatting | bytes 262144

commit v4 on v2

--- a/solution.py
+++ b/solution.py
@@ -240,7 +240,8 @@
         return 0
 
     pass1(0, True)
-    lax.fori_loop(1, NC, lambda c, _: pass1(c, False), 0)
+    for c in range(1, NC):
+        pass1(c, False)
 
     for d in range(1, NZ):
         remote(SM, SR.at[d], ds_.at[d], dr.at[d], zpeer(d)).wait_recv()

time: 43.7 us -> 43.5 us (level)
  no operation moved by 1% of the time
where the time goes in v4:
time: 43.5 us; the launch traced here: 43.4 us
  Pallas kernels  40.8 us (94%)
  local copies, waits for them, and re-layouts  1.94 us (4%)
  between operations  0.64 us (1%)
    pallas_call x1, Pallas kernels, body(): pl.pallas_call(lambda *refs: kernel(NT, *refs), out_shape=(V((R, D), F32)...  40.8 us
    unnamed x3, local copies, waits for them, and re-layouts  1.94 us

profile of v4, /device:TPU:1, one launch (start us, length us, event | category | flops | bytes accessed | tf_op | source)
XLA Modules:
  0.0 43.4 jit_solution(10261343344261789731)
XLA Ops:
  0.6 40.8 %shard_map.76 = (f32[16,1024]{1,0:T(8,128)S(1)}, f32[256,128]{1,0:T(8,128)S(1)}, f32[256,128]{1,0:T(8,128)S(1)}) custom-call(bf16[16,1024]{1,0:T(8,128)(2,1)} %refs_0_.1, bf16[256,1024]{1,0:T(8,128)(2,1)} %refs_1_.1, bf16[256,1024]{1,0:T(8,128)(2,1)} %refs_2_.1, bf16[16,1024]{1,0:T(8,128)(2,1)} %refs_3_.1, s32[4,128]{1,0:T(4,128)} %bitcast.1), custom_call_target="tpu_custom_call" | custom-call | tf_op jit(solution)/shard_map/pallas_call | solution.py:377
  41.5 0.6 %copy.11 = f32[16,1024]{1,0:T(8,128)} copy(f32[16,1024]{1,0:T(8,128)S(1)} %get-tuple-element.3) | data formatting | bytes 131072
  42.1 0.7 %copy.12 = f32[256,128]{1,0:T(8,128)} copy(f32[256,128]{1,0:T(8,128)S(1)} %get-tuple-element.4) | data formatting | bytes 262144
  42.8 0.7 %copy.13 = f32[256,128]{1,0:T(8,128)} copy(f32[256,128]{1,0:T(8,128)S(1)} %get-tuple-element.5) | data formatting | bytes 262144
